TPU v7x, 32 devices: a whole 2x2x4 slice. The times are simulated.
32 devices in a mesh: groups: 2 (over y), pole: 2 (over core), grow: 2 (over x), gcol: 4 (over z).
Axes of the slice: x: 2, y: 2, z: 4, core: 2. Of those that a mesh axis runs over, the one named last changes fastest.
Arguments:
- inverse_block: bfloat16 [8, 2, 1024, 1024], P(('groups', 'pole'), None, 'grow', 'gcol'), parts along dimension 0, may hold values from -0.125 to 0.125
- lower_panel: bfloat16 [8, 2, 1024, 512], P(('groups', 'pole'), None, 'grow', 'gcol'), parts along dimension 0, may hold values from -6 to 6
- tile_pattern: int32 [8, 8], P('groups'), parts along dimension 0, may hold values 0 or 1
- diag_inverse: float32 [8, 2, 4, 128, 128], P(('groups', 'pole'), None, 'gcol'), parts along dimension 0, may hold values from -6 to 6
- pole_weight: float32 [8, 2], P(('groups', 'pole')), parts along dimension 0, may hold values from -4 to 4
Outputs:
- density_panel: float32 [2048, 512], P(('groups', 'grow'), 'gcol'), parts along dimension 0
- density_diag: float32 [8, 128, 128], P(('groups', 'gcol')), parts along dimension 0
There are 2 independent parts, one for each index of `groups`. A program takes and returns all parts, laid end to end along the dimension named above; each array names one. Nothing has to cross between parts.
All inputs are finite; a program needn't handle non-finite values.
Results may differ from a plain program's by a relative error of at most 0.0029.
Values may be sent and summed in bfloat16 or wider, within the bound.
A program may use at most 64 MiB of HBM per device.

v0:
```python
import jax
import jax.numpy as jnp
from jax import lax
from jax.sharding import PartitionSpec as P

TILE = 128


def batch_dot(left, right):
    return jnp.einsum("pij,pjk->pik", left, right, preferred_element_type=jnp.float32)


def negated_product(left, right):
    real_part = batch_dot(left[:, 1], right[:, 1]) - batch_dot(left[:, 0], right[:, 0])
    imag_part = -(batch_dot(left[:, 0], right[:, 1]) + batch_dot(left[:, 1], right[:, 0]))
    return jnp.stack([real_part, imag_part], axis=1)


def block_quad(left, right):
    return jnp.einsum("pika,pikb->pkab", left, right, preferred_element_type=jnp.float32)


def weighted(weight_re, weight_im, values):
    return jnp.sum(weight_re * values[:, 0] - weight_im * values[:, 1], axis=0)


def shards(inverse_block, lower_panel, tile_pattern, diag_inverse, pole_weight):
    row_index = lax.axis_index("grow")
    col_index = lax.axis_index("gcol")
    local_poles = inverse_block.shape[0]
    local_rows = inverse_block.shape[2]
    width = lower_panel.shape[3]
    own_sups = width // TILE
    row_tiles = local_rows // TILE
    pattern_here = lax.dynamic_slice(
        tile_pattern, (col_index * own_sups, row_index * row_tiles), (own_sups, row_tiles)
    )
    tile_mask = jnp.repeat(jnp.repeat(pattern_here.T, TILE, axis=0), TILE, axis=1).astype(
        jnp.bfloat16
    )
    masked = lower_panel * tile_mask
    all_rows = lax.all_gather(masked, "grow", axis=2, tiled=True)
    solved = negated_product(lax.all_gather(inverse_block, "gcol", axis=3, tiled=True), all_rows)
    rounded = solved.astype(jnp.bfloat16)
    shaped_lower = masked.reshape(local_poles, 2, local_rows, own_sups, TILE)
    shaped_solved = rounded.reshape(local_poles, 2, local_rows, own_sups, TILE)
    q_re = block_quad(shaped_lower[:, 0], shaped_solved[:, 0]) - block_quad(
        shaped_lower[:, 1], shaped_solved[:, 1]
    )
    q_im = block_quad(shaped_lower[:, 0], shaped_solved[:, 1]) + block_quad(
        shaped_lower[:, 1], shaped_solved[:, 0]
    )
    quad_pair = jnp.stack([q_re, q_im], axis=1)
    weight_re = pole_weight[:, 0][:, None, None, None]
    weight_im = pole_weight[:, 1][:, None, None, None]
    panel_term = weighted(
        pole_weight[:, 0][:, None, None], pole_weight[:, 1][:, None, None], solved
    )
    quad_total = lax.psum(quad_pair, "grow")
    diag_block = diag_inverse - quad_total
    diag_term = weighted(weight_re, weight_im, diag_block)
    density_panel, density_diag = lax.psum((panel_term, diag_term), "pole")
    return (density_panel, density_diag)


def solution(mesh):
    placed = (
        P(("groups", "pole"), None, "grow", "gcol"),
        P(("groups", "pole"), None, "grow", "gcol"),
        P("groups", None),
        P(("groups", "pole"), None, "gcol", None, None),
        P(("groups", "pole"), None),
    )
    return jax.shard_map(
        shards,
        mesh=mesh,
        in_specs=placed,
        out_specs=(P(("groups", "grow"), "gcol"), P(("groups", "gcol"), None, None)),
        check_vma=False,
    )
```

profile of v0, /device:TPU:0, one launch (start us, length us, event | category | flops | bytes accessed | tf_op | source)
XLA Modules:
  0.0 178.7 jit_solution(16003399375845794941)
XLA Ops:
  7.2 0.0 copy-start.1
  7.2 0.0 all-gather.3.cloned.1.call-start
  7.2 0.8 convert_bitcast_fusion
  8.0 0.1 broadcast_bitcast_fusion
  8.1 1.2 copy.10
  9.3 0.8 broadcast_multiply_fusion
  10.2 0.0 all-gather.3.cloned.1.call-update
  10.2 0.0 all-gather.5.cloned.1.call-start
  10.2 2.3 %copy.11 = bf16[2,2,512,256]{3,2,0,1:T(8,128)(2,1)} copy(bf16[2,2,512,256]{3,2,1,0:T(8,128)(2,1)} %param.5) | data formatting | bytes 2097152 | tf_op args[0]
  12.5 0.0 all-gather.5.cloned.1.call-update
  12.5 0.0 all-reduce.4.cloned.1.call-start
  12.6 0.0 copy-done.1
  12.6 0.2 slice_reduce_fusion.1
  12.8 21.5 %all-gather.3.cloned.1.call-done = bf16[2,2,1024,128]{2,3,0,1:T(8,128)(2,1)} async-done(((bf16[2,2,512,128]{2,3,0,1:T(8,128)(2,1)}), bf16[2,2,1024,128]{2,3,0,1:T(8,128)(2,1)}) %all-gather.3.cloned.1.call-update) | async-done | bytes 1048592 | tf_op jit(solution)/shard_map/all_gather | solution.py:42
  34.3 0.0 copy-start.3
  34.3 82.2 %all-gather.5.cloned.1.call-done = bf16[2,2,512,1024]{3,2,0,1:T(8,128)(2,1)} async-done(((bf16[2,2,512,256]{3,2,0,1:T(8,128)(2,1)}), bf16[2,2,512,1024]{3,2,0,1:T(8,128)(2,1)}) %all-gather.5.cloned.1.call-update) | async-done | bytes 4194320 | tf_op jit(solution)/shard_map/all_gather | solution.py:43
  116.5 0.0 copy-start.2
  116.5 2.7 %fusion.1 = f32[2,128,512]{2,1,0:T(8,128)S(1)} fusion(bf16[2,2,512,1024]{3,2,0,1:T(8,128)(2,1)} %all-gather.5.cloned.1.call-done, bf16[2,2,1024,128]{2,3,0,1:T(8,128)(2,1)} %all-gather.3.cloned.1.call-done), kind=kOutput, calls=%fused_computation.3 | convolution fusion | flops 268435456 | bytes 3145728 | tf_op jit(solution)/shard_map/pij,pjk->pik/dot_general | solution.py:10
  119.2 2.6 %fusion.4 = f32[2,128,512]{2,1,0:T(8,128)S(1)} fusion(f32[2,128,512]{2,1,0:T(8,128)S(1)} %fusion.1, bf16[2,2,512,1024]{3,2,0,1:T(8,128)(2,1)} %all-gather.5.cloned.1.call-done, bf16[2,2,1024,128]{2,3,0,1:T(8,128)(2,1)} %all-gather.3.cloned.1.call-done), kind=kOutput, calls=%fused_computation.6 | convolution fusion | flops 268566528 | bytes 3670016 | tf_op jit(solution)/shard_map/pij,pjk->pik/dot_general | solution.py:10
  121.9 0.2 fusion.10
  122.1 0.0 copy-done.3
  122.1 0.0 copy-done.2
  122.1 0.8 fusion
  122.9 0.0 copy-start
  123.0 1.6 subtract_reduce_fusion
  124.5 0.2 fusion.9
  124.8 0.2 fusion.7
  125.0 0.2 fusion.8
  125.2 0.7 pad_maximum_fusion
  126.0 0.0 all-reduce.4.cloned.1.call-update
  126.0 0.0 all-reduce.6.cloned.1.call-start
  126.0 21.5 %all-reduce.4.cloned.1.call-done = f32[2,2,1,128,128]{4,3,0,2,1:T(8,128)} async-done(((f32[2,2,1,128,128]{4,3,0,2,1:T(8,128)}), f32[2,2,1,128,128]{4,3,0,2,1:T(8,128)}) %all-reduce.4.cloned.1.call-update) | async-done | bytes 262160 | tf_op jit(solution)/shard_map/psum | solution.py:59
  147.5 0.0 copy-done
  147.5 1.0 copy_subtract_fusion
  148.5 0.7 fusion.13
  149.2 0.0 all-reduce.6.cloned.1.call-update
  149.3 19.7 %all-reduce.6.cloned.1.call-done = (f32[512,128]{0,1:T(8,128)}, f32[1,128,128]{2,1,0:T(8,128)}) async-done(((f32[512,128]{0,1:T(8,128)}, f32[1,128,128]{2,1,0:T(8,128)}), (f32[512,128]{0,1:T(8,128)}, f32[1,128,128]{2,1,0:T(8,128)})) %all-reduce.6.cloned.1.call-update) | async-done | bytes 327696 | tf_op jit(solution)/shard_map/psum | solution.py:62
  168.9 1.8 copy.13
  170.7 1.5 copy.18
  (1 shorter events, 0.0 us)
Async XLA Ops:
  7.2 5.4 %copy-start.1 = (f32[2,2]{1,0:T(2,128)S(1)}, f32[2,2]{1,0:T(2,128)}, u32[]{:S(2)}) copy-start(f32[2,2]{1,0:T(2,128)} %param.9) | copy-start | bytes 52
  7.2 27.2 %all-gather.3.cloned.1.call-start = ((), (), s32[]{:S(2)}) async-start(), calls=%async_computation | async-start | bytes 1572864 | tf_op jit(solution)/shard_map/all_gather | solution.py:42
  10.2 106.3 %all-gather.5.cloned.1.call-start = ((), (), s32[]{:S(2)}) async-start(), calls=%async_computation.1 | async-start | bytes 5242880 | tf_op jit(solution)/shard_map/all_gather | solution.py:43
  12.5 135.0 %all-reduce.4.cloned.1.call-start = ((), (), s32[]{:S(2)}) async-start(), calls=%async_computation.2 | async-start | bytes 524288 | tf_op jit(solution)/shard_map/psum | solution.py:59
  34.3 87.8 %copy-start.3 = (bf16[2,2,1024,128]{2,3,0,1:T(8,128)(2,1)S(1)}, bf16[2,2,1024,128]{2,3,0,1:T(8,128)(2,1)}, u32[]{:S(2)}) copy-start(bf16[2,2,1024,128]{2,3,0,1:T(8,128)(2,1)} %all-gather.3.cloned.1.call-done) | copy-start | bytes 3145732
  116.5 5.6 %copy-start.2 = (bf16[2,2,512,1024]{3,2,0,1:T(8,128)(2,1)S(1)}, bf16[2,2,512,1024]{3,2,0,1:T(8,128)(2,1)}, u32[]{:S(2)}) copy-start(bf16[2,2,512,1024]{3,2,0,1:T(8,128)(2,1)} %all-gather.5.cloned.1.call-done) | copy-start | bytes 12582916
  122.9 24.6 %copy-start = (f32[2,2,1,128,128]{4,3,2,1,0:T(8,128)S(1)}, f32[2,2,1,128,128]{4,3,2,1,0:T(8,128)}, u32[]{:S(2)}) copy-start(f32[2,2,1,128,128]{4,3,2,1,0:T(8,128)} %param.8) | copy-start | bytes 786436
  126.0 42.9 %all-reduce.6.cloned.1.call-start = ((), (), s32[]{:S(2)}) async-start(), calls=%async_computation.3 | async-start | bytes 655360 | tf_op jit(solution)/shard_map/psum | solution.py:62
Sparse Core Ops, SparseCore 0:
  10.3 23.9 all-gather.2
  35.9 80.5 all-gather.4
  126.1 21.3 all-reduce.3
  150.5 18.4 all-reduce.5
where the time goes:
time: 179 us
  waiting for transfers between devices  145 us (81%)
  between operations  13.9 us (8%)
  matrix products  8.65 us (5%)
  local copies, waits for them, and re-layouts  7.06 us (4%)
  other arithmetic  4.07 us (2%)
    all_gather x1, waiting for transfers between devices, shards(): lax.all_gather(inverse_block, 'gcol', axis=3, tiled=True)  82.2 us
    all_gather x1, waiting for transfers between devices, shards(): all_rows = lax.all_gather(masked, 'grow', axis=2, tiled=True)  21.5 us
    psum x1, waiting for transfers between devices, shards(): quad_total = lax.psum(quad_pair, 'grow')  21.5 us
    psum x1, waiting for transfers between devices, shards(): density_panel, density_diag = lax.psum((panel_term, diag_term), 'pole')  19.7 us
    dot_general x4, matrix products, batch_dot(): jnp.einsum('pij,pjk->pik', left, right, preferred_element_type=jnp.float32)  7.75 us
    unnamed x12, local copies, waits for them, and re-layouts  6.81 us
  transfers between devices with their start and end apart: 4, of which 4 were waited for; matrix products, arithmetic and copies ran while one was open for 1% of the time, Pallas kernels for 0%

commit v1 on v0

v1 whole, which is shorter than its diff:
```python
import functools

import jax
import jax.numpy as jnp
from jax import lax
from jax.experimental import pallas as pl
from jax.experimental.pallas import tpu as pltpu
from jax.sharding import PartitionSpec as P

TILE = 128
MESH = pl.DeviceIdType.MESH


def kernel(
    row_count,
    chunk,
    pattern_ref,
    weight_ref,
    inverse_ref,
    lower_ref,
    diag_ref,
    panel_out,
    diag_out,
    panels,
    inverse_next,
    total,
    panel_send,
    panel_recv,
    final,
    final_recv,
    quad,
    quad_send,
    quad_recv,
    shares,
    m_send,
    m_recv,
    x_send,
    x_recv,
    g_send,
    g_recv,
    p_send,
    p_recv,
    c_send,
    c_recv,
    q_send,
    q_recv,
    s_send,
    s_recv,
):
    poles, _, rows, half = inverse_ref.shape
    chunks = rows // chunk
    row_tiles = rows // TILE
    row = lax.axis_index("grow")
    col = lax.axis_index("gcol")
    core = lax.axis_index("pole")
    high, low = col // 2, col % 2
    inner = jnp.where(row == high, 0, 1)

    def to_high(step):
        return {"gcol": lax.rem(high + step, row_count) * 2 + low}

    def to_row(step):
        return {"grow": lax.rem(row + step, row_count)}

    def send_m(pole, step):
        return pltpu.make_async_remote_copy(
            src_ref=panels.at[0, high, pole],
            dst_ref=panels.at[0, high, pole],
            send_sem=m_send.at[step - 1, pole],
            recv_sem=m_recv.at[step - 1, pole],
            device_id=to_high(step),
            device_id_type=MESH,
        )

    def send_x(pole, step, across):
        sup = lax.rem(high + row_count - step, row_count)
        return pltpu.make_async_remote_copy(
            src_ref=panels.at[0, sup, pole],
            dst_ref=panels.at[1, sup, pole],
            send_sem=x_send.at[across - 1, step, pole],
            recv_sem=x_recv.at[step, pole],
            device_id=to_row(across),
            device_id_type=MESH,
        )

    def send_g(index):
        cut = pl.ds(pl.multiple_of(index * chunk, chunk), chunk)
        return pltpu.make_async_remote_copy(
            src_ref=inverse_ref.at[:, :, cut, :],
            dst_ref=inverse_next.at[:, :, cut, :],
            send_sem=g_send.at[index],
            recv_sem=g_recv.at[index],
            device_id={"gcol": high * 2 + 1 - low},
            device_id_type=MESH,
        )

    def send_p(index, step):
        return pltpu.make_async_remote_copy(
            src_ref=panel_send.at[index, lax.rem(high + step, row_count)],
            dst_ref=panel_recv.at[index, step - 1],
            send_sem=p_send.at[index, step - 1],
            recv_sem=p_recv.at[index, step - 1],
            device_id=to_high(step),
            device_id_type=MESH,
        )

    def send_c(index):
        return pltpu.make_async_remote_copy(
            src_ref=final.at[index],
            dst_ref=final_recv.at[index],
            send_sem=c_send.at[index],
            recv_sem=c_recv.at[index],
            device_id={"pole": 1 - core},
            device_id_type=MESH,
        )

    def send_q(step):
        return pltpu.make_async_remote_copy(
            src_ref=quad_send.at[lax.rem(high + step, row_count)],
            dst_ref=quad_recv.at[step - 1],
            send_sem=q_send.at[step - 1],
            recv_sem=q_recv.at[step - 1],
            device_id=to_high(step),
            device_id_type=MESH,
        )

    others = [(across, flip) for across in range(row_count) for flip in range(2) if (across, flip) != (0, 0)]

    def send_s(which):
        across, flip = others[which]
        return pltpu.make_async_remote_copy(
            src_ref=shares.at[row, core],
            dst_ref=shares.at[row, core],
            send_sem=s_send.at[which],
            recv_sem=s_recv.at[which],
            device_id={"grow": lax.rem(row + across, row_count), "pole": lax.rem(core + flip, 2)},
            device_id_type=MESH,
        )

    barrier = pltpu.get_barrier_semaphore()
    peers = [{"gcol": high * 2 + 1 - low}]
    peers += [to_high(step) for step in range(1, row_count)]
    peers += [
        {"grow": lax.rem(row + across, row_count), "pole": lax.rem(core + flip, 2)} for across, flip in others
    ]
    for peer in peers:
        pl.semaphore_signal(barrier, inc=1, device_id=peer, device_id_type=MESH)

    for tile in range(row_tiles):
        present = pattern_ref[col, row * row_tiles + tile].astype(jnp.float32).astype(jnp.bfloat16)
        cut = slice(tile * TILE, (tile + 1) * TILE)
        for pole in range(poles):
            panels[0, high, pole, :, cut, :] = lower_ref[pole, :, cut, :] * present

    pl.semaphore_wait(barrier, len(peers))

    for pole in range(poles):
        for step in range(1, row_count):
            send_m(pole, step).start()

    @pl.when(row == high)
    def _():
        for pole in range(poles):
            for across in range(1, row_count):
                send_x(pole, 0, across).start()

    for index in range(chunks):
        send_g(index).start()

    quad[...] = jnp.zeros_like(quad)

    for pole in range(poles):
        for step in range(1, row_count):
            send_m(pole, step).wait_recv()

            @pl.when(row == high)
            def _():
                for across in range(1, row_count):
                    send_x(pole, step, across).start()

    @pl.when(row != high)
    def _():
        for pole in range(poles):
            for step in range(row_count):
                send_x(pole, step, 1).wait_recv()

    def finish(index):
        cut = pl.ds(pl.multiple_of(index * chunk, chunk), chunk)
        value = total[high, cut, :]
        for step in range(1, row_count):
            send_p(index, step).wait_recv()
            value = value + panel_recv[index, step - 1].astype(jnp.float32)
        final[index] = value
        send_c(index).start()

    own_rows = pl.ds(pl.multiple_of(low * half, half), half)
    next_rows = pl.ds(pl.multiple_of((1 - low) * half, half), half)

    def dot(left, right):
        return jnp.dot(left, right, preferred_element_type=jnp.float32)

    def work(index, carry):
        cut = pl.ds(pl.multiple_of(index * chunk, chunk), chunk)
        send_g(index).wait_recv()
        for sup in range(row_count):
            summed = None
            for pole in range(poles):
                m_own = jnp.concatenate(
                    [panels[inner, sup, pole, 0, own_rows, :], panels[inner, sup, pole, 1, own_rows, :]], axis=1
                )
                m_next = jnp.concatenate(
                    [panels[inner, sup, pole, 0, next_rows, :], panels[inner, sup, pole, 1, next_rows, :]], axis=1
                )
                by_re = dot(inverse_ref[pole, 0, cut, :], m_own) + dot(inverse_next[pole, 0, cut, :], m_next)
                by_im = dot(inverse_ref[pole, 1, cut, :], m_own) + dot(inverse_next[pole, 1, cut, :], m_next)
                solved_re = by_im[:, TILE:] - by_re[:, :TILE]
                solved_im = -(by_re[:, TILE:] + by_im[:, :TILE])
                w_re, w_im = weight_ref[pole, 0], weight_ref[pole, 1]
                scaled_re = w_re * solved_re - w_im * solved_im
                scaled_im = w_re * solved_im + w_im * solved_re
                summed = scaled_re if summed is None else summed + scaled_re
                stacked = jnp.concatenate([-scaled_re, scaled_im], axis=0)
                upper = stacked.astype(jnp.bfloat16)
                rest = (stacked - upper.astype(jnp.float32)).astype(jnp.bfloat16)
                m_rows = jnp.concatenate(
                    [panels[0, sup, pole, 0, cut, :], panels[0, sup, pole, 1, cut, :]], axis=0
                )
                quad[sup] += lax.dot_general(
                    m_rows,
                    jnp.concatenate([upper, rest], axis=1),
                    (((0,), (0,)), ((), ())),
                    preferred_element_type=jnp.float32,
                )
            total[sup, cut, :] = summed
            panel_send[index, sup] = summed.astype(jnp.bfloat16)
        for step in range(1, row_count):
            send_p(index, step).start()

        @pl.when(index >= 1)
        def _():
            finish(index - 1)

        return carry

    lax.fori_loop(0, chunks, work, 0)

    for sup in range(row_count):
        quad_send[sup] = quad[sup, :, :TILE] + quad[sup, :, TILE:]
    for step in range(1, row_count):
        send_q(step).start()
    once = jnp.where(row == 0, 1.0, 0.0)
    share = quad_send[high]
    for pole in range(poles):
        share = share + (once * weight_ref[pole, 0]) * diag_ref[pole, 0, 0]
        share = share - (once * weight_ref[pole, 1]) * diag_ref[pole, 1, 0]
    finish(chunks - 1)
    for step in range(1, row_count):
        send_q(step).wait_recv()
        share = share + quad_recv[step - 1]
    shares[row, core] = share
    for which in range(len(others)):
        send_s(which).start()
    for index in range(chunks):
        send_c(index).wait_recv()
        panel_out[index * chunk : (index + 1) * chunk, :] = final[index] + final_recv[index]
    for which in range(len(others)):
        send_s(which).wait_recv()
    value = shares[0, 0]
    for at in range(1, 2 * row_count):
        value = value + shares[at // 2, at % 2]
    diag_out[0] = value

    for pole in range(poles):
        for step in range(1, row_count):
            send_m(pole, step).wait_send()

    @pl.when(row == high)
    def _():
        for pole in range(poles):
            for step in range(row_count):
                for across in range(1, row_count):
                    send_x(pole, step, across).wait_send()

    for index in range(chunks):
        send_g(index).wait_send()
        send_c(index).wait_send()
        for step in range(1, row_count):
            send_p(index, step).wait_send()
    for step in range(1, row_count):
        send_q(step).wait_send()
    for which in range(len(others)):
        send_s(which).wait_send()


def shards(row_count, inverse_block, lower_panel, tile_pattern, diag_inverse, pole_weight):
    poles, _, rows, half = inverse_block.shape
    chunk = 128
    chunks = rows // chunk
    vmem = pl.BlockSpec(memory_space=pltpu.VMEM)
    smem = pl.BlockSpec(memory_space=pltpu.SMEM)
    dma = pltpu.SemaphoreType.DMA
    bf16, f32 = jnp.bfloat16, jnp.float32
    steps = row_count - 1
    flops = 2 * poles * rows * half * 2 * TILE * row_count * 5
    return pl.pallas_call(
        functools.partial(kernel, row_count, chunk),
        out_shape=(
            jax.ShapeDtypeStruct((rows, TILE), f32),
            jax.ShapeDtypeStruct((1, TILE, TILE), f32),
        ),
        in_specs=[smem, smem, vmem, vmem, vmem],
        out_specs=(vmem, vmem),
        scratch_shapes=[
            pltpu.VMEM((2, row_count, poles, 2, rows, TILE), bf16),
            pltpu.VMEM((poles, 2, rows, half), bf16),
            pltpu.VMEM((row_count, rows, TILE), f32),
            pltpu.VMEM((chunks, row_count, chunk, TILE), bf16),
            pltpu.VMEM((chunks, steps, chunk, TILE), bf16),
            pltpu.VMEM((chunks, chunk, TILE), f32),
            pltpu.VMEM((chunks, chunk, TILE), f32),
            pltpu.VMEM((row_count, TILE, 2 * TILE), f32),
            pltpu.VMEM((row_count, TILE, TILE), f32),
            pltpu.VMEM((steps, TILE, TILE), f32),
            pltpu.VMEM((row_count, 2, TILE, TILE), f32),
            dma((steps, poles)),
            dma((steps, poles)),
            dma((steps, row_count, poles)),
            dma((row_count, poles)),
            dma((chunks,)),
            dma((chunks,)),
            dma((chunks, steps)),
            dma((chunks, steps)),
            dma((chunks,)),
            dma((chunks,)),
            dma((steps,)),
            dma((steps,)),
            dma((2 * row_count - 1,)),
            dma((2 * row_count - 1,)),
        ],
        compiler_params=pltpu.CompilerParams(
            collective_id=0, has_side_effects=True, vmem_limit_bytes=40 * 1024 * 1024
        ),
        cost_estimate=pl.CostEstimate(flops=flops, bytes_accessed=4 * 1024 * 1024, transcendentals=0),
    )(tile_pattern, pole_weight, inverse_block, lower_panel, diag_inverse)


def solution(mesh):
    placed = (
        P(("groups", "pole"), None, "grow", "gcol"),
        P(("groups", "pole"), None, "grow", "gcol"),
        P("groups", None),
        P(("groups", "pole"), None, "gcol", None, None),
        P(("groups", "pole"), None),
    )
    return jax.shard_map(
        functools.partial(shards, mesh.shape["grow"]),
        mesh=mesh,
        in_specs=placed,
        out_specs=(P(("groups", "grow"), "gcol"), P(("groups", "gcol"), None, None)),
        check_vma=False,
    )
```

time: 179 us -> 61 us (0.34)
  the two profiles are of different devices: /device:TPU:0 before, /device:TPU:13 now
where the time goes in v1:
time: 61 us; the launch traced here: 60.7 us
  Pallas kernels  54.2 us (89%)
  local copies, waits for them, and re-layouts  5.9 us (10%)
  between operations  0.65 us (1%)
    pallas_call x1, Pallas kernels, shards(): pl.pallas_call(functools.partial(kernel, row_count, chunk), out_shape=(ja...  54.2 us
    unnamed x12, local copies, waits for them, and re-layouts  5.9 us

profile of v1, /device:TPU:13, one launch (start us, length us, event | category | flops | bytes accessed | tf_op | source)
XLA Modules:
  0.0 60.7 jit_solution(10080389723704398281)
XLA Ops:
  0.6 0.0 copy-start
  0.6 1.2 %copy-done = bf16[2,2,512,256]{3,2,1,0:T(8,128)(2,1)S(1)} copy-done((bf16[2,2,512,256]{3,2,1,0:T(8,128)(2,1)S(1)}, bf16[2,2,512,256]{3,2,1,0:T(8,128)(2,1)}, u32[]{:S(2)}) %copy-start) | copy-done | bytes 1048600
  1.9 0.0 copy-start.1
  1.9 1.0 %copy-done.1 = bf16[2,2,512,128]{3,2,1,0:T(8,128)(2,1)S(1)} copy-done((bf16[2,2,512,128]{3,2,1,0:T(8,128)(2,1)S(1)}, bf16[2,2,512,128]{3,2,1,0:T(8,128)(2,1)}, u32[]{:S(2)}) %copy-start.1) | copy-done | bytes 524312
  2.9 0.0 copy-start.2
  2.9 0.9 %copy-done.2 = f32[2,2,1,128,128]{4,3,2,1,0:T(8,128)S(1)} copy-done((f32[2,2,1,128,128]{4,3,2,1,0:T(8,128)S(1)}, f32[2,2,1,128,128]{4,3,2,1,0:T(8,128)}, u32[]{:S(2)}) %copy-start.2) | copy-done | bytes 262168
  3.8 0.0 copy-start.3
  3.9 0.7 %copy-done.3 = s32[4,8]{1,0:T(4,128)S(1)} copy-done((s32[4,8]{1,0:T(4,128)S(1)}, s32[4,8]{1,0:T(4,128)}, u32[]{:S(2)}) %copy-start.3) | copy-done | bytes 152
  4.5 0.0 copy-start.4
  4.5 0.7 %copy-done.4 = f32[2,2]{1,0:T(2,128)S(1)} copy-done((f32[2,2]{1,0:T(2,128)S(1)}, f32[2,2]{1,0:T(2,128)}, u32[]{:S(2)}) %copy-start.4) | copy-done | bytes 40
  5.2 54.2 %shard_map.68 = (f32[512,128]{1,0:T(8,128)S(1)}, f32[1,128,128]{2,1,0:T(8,128)S(1)}) custom-call(s32[4,8]{1,0:T(4,128)S(1)} %copy-done.3, f32[2,2]{1,0:T(2,128)S(1)} %copy-done.4, bf16[2,2,512,256]{3,2,1,0:T(8,128)(2,1)S(1)} %copy-done, bf16[2,2,512,128]{3,2,1,0:T(8,128)(2,1)S(1)} %copy-done.1, f32[2,2,1,128,128]{4,3,2,1,0:T(8,128)S(1)} %copy-done.2), custom_call_target="tpu_custom_call" | custom-call | flops 1342177280 | bytes 4194304 | tf_op jit(solution)/shard_map/pallas_call | solution.py:305
  59.4 0.7 %copy.9 = f32[512,128]{1,0:T(8,128)} copy(f32[512,128]{1,0:T(8,128)S(1)} %get-tuple-element.4) | data formatting | bytes 524288
  60.1 0.6 %copy.10 = f32[1,128,128]{2,1,0:T(8,128)} copy(f32[1,128,128]{2,1,0:T(8,128)S(1)} %get-tuple-element.5) | data formatting | bytes 131072
Async XLA Ops:
  0.6 1.2 %copy-start = (bf16[2,2,512,256]{3,2,1,0:T(8,128)(2,1)S(1)}, bf16[2,2,512,256]{3,2,1,0:T(8,128)(2,1)}, u32[]{:S(2)}) copy-start(bf16[2,2,512,256]{3,2,1,0:T(8,128)(2,1)} %inverse_ref.1) | copy-start | bytes 3145732
  1.9 1.0 %copy-start.1 = (bf16[2,2,512,128]{3,2,1,0:T(8,128)(2,1)S(1)}, bf16[2,2,512,128]{3,2,1,0:T(8,128)(2,1)}, u32[]{:S(2)}) copy-start(bf16[2,2,512,128]{3,2,1,0:T(8,128)(2,1)} %lower_ref.1) | copy-start | bytes 1572868
  2.9 0.9 %copy-start.2 = (f32[2,2,1,128,128]{4,3,2,1,0:T(8,128)S(1)}, f32[2,2,1,128,128]{4,3,2,1,0:T(8,128)}, u32[]{:S(2)}) copy-start(f32[2,2,1,128,128]{4,3,2,1,0:T(8,128)} %diag_ref.1) | copy-start | bytes 786436
  3.8 0.7 %copy-start.3 = (s32[4,8]{1,0:T(4,128)S(1)}, s32[4,8]{1,0:T(4,128)}, u32[]{:S(2)}) copy-start(s32[4,8]{1,0:T(4,128)} %pattern_ref.1) | copy-start | bytes 388
  4.5 0.7 %copy-start.4 = (f32[2,2]{1,0:T(2,128)S(1)}, f32[2,2]{1,0:T(2,128)}, u32[]{:S(2)}) copy-start(f32[2,2]{1,0:T(2,128)} %weight_ref.1) | copy-start | bytes 52

commit v2 on v1

--- a/solution.py
+++ b/solution.py
@@ -14,13 +14,20 @@
 def kernel(
     row_count,
     chunk,
+    pattern_hbm,
+    weight_hbm,
+    inverse_hbm,
+    lower_hbm,
+    diag_hbm,
+    panel_out,
+    diag_out,
     pattern_ref,
     weight_ref,
     inverse_ref,
     lower_ref,
     diag_ref,
-    panel_out,
-    diag_out,
+    load_sem,
+    early,
     panels,
     inverse_next,
     total,
@@ -62,23 +69,30 @@
     def to_row(step):
         return {"grow": lax.rem(row + step, row_count)}
 
-    def send_m(pole, step):
-        return pltpu.make_async_remote_copy(
-            src_ref=panels.at[0, high, pole],
-            dst_ref=panels.at[0, high, pole],
-            send_sem=m_send.at[step - 1, pole],
-            recv_sem=m_recv.at[step - 1, pole],
+    def piece(at):
+        return at // 2, pl.ds((at % 2) * (rows // 2), rows // 2)
+
+    pieces = 2 * poles
+
+    def send_m(at, step):
+        pole, part = piece(at)
+        return pltpu.make_async_remote_copy(
+            src_ref=panels.at[0, high, pole, :, part],
+            dst_ref=panels.at[0, high, pole, :, part],
+            send_sem=m_send.at[step - 1, at],
+            recv_sem=m_recv.at[step - 1, at],
             device_id=to_high(step),
             device_id_type=MESH,
         )
 
-    def send_x(pole, step, across):
+    def send_x(at, step, across):
+        pole, part = piece(at)
         sup = lax.rem(high + row_count - step, row_count)
         return pltpu.make_async_remote_copy(
-            src_ref=panels.at[0, sup, pole],
-            dst_ref=panels.at[1, sup, pole],
-            send_sem=x_send.at[across - 1, step, pole],
-            recv_sem=x_recv.at[step, pole],
+            src_ref=panels.at[0, sup, pole, :, part],
+            dst_ref=panels.at[1, sup, pole, :, part],
+            send_sem=x_send.at[across - 1, step, at],
+            recv_sem=x_recv.at[step, at],
             device_id=to_row(across),
             device_id_type=MESH,
         )
@@ -86,7 +100,7 @@
     def send_g(index):
         cut = pl.ds(pl.multiple_of(index * chunk, chunk), chunk)
         return pltpu.make_async_remote_copy(
-            src_ref=inverse_ref.at[:, :, cut, :],
+            src_ref=inverse_hbm.at[:, :, cut, :],
             dst_ref=inverse_next.at[:, :, cut, :],
             send_sem=g_send.at[index],
             recv_sem=g_recv.at[index],
@@ -146,6 +160,23 @@
     for peer in peers:
         pl.semaphore_signal(barrier, inc=1, device_id=peer, device_id_type=MESH)
 
+    loads = [
+        pltpu.make_async_copy(source, target, load_sem.at[at])
+        for at, (source, target) in enumerate(
+            (
+                (pattern_hbm, pattern_ref),
+                (lower_hbm, lower_ref),
+                (weight_hbm, weight_ref),
+                (inverse_hbm, inverse_ref),
+                (diag_hbm, diag_ref),
+            )
+        )
+    ]
+    for load in loads:
+        load.start()
+    loads[0].wait()
+    loads[1].wait()
+
     for tile in range(row_tiles):
         present = pattern_ref[col, row * row_tiles + tile].astype(jnp.float32).astype(jnp.bfloat16)
         cut = slice(tile * TILE, (tile + 1) * TILE)
@@ -154,35 +185,41 @@
 
     pl.semaphore_wait(barrier, len(peers))
 
-    for pole in range(poles):
+    for at in range(pieces):
         for step in range(1, row_count):
-            send_m(pole, step).start()
+            send_m(at, step).start()
 
     @pl.when(row == high)
     def _():
-        for pole in range(poles):
+        for at in range(pieces):
             for across in range(1, row_count):
-                send_x(pole, 0, across).start()
-
-    for index in range(chunks):
+                send_x(at, 0, across).start()
+
+    ahead = 1
+    for index in range(ahead):
         send_g(index).start()
 
     quad[...] = jnp.zeros_like(quad)
-
-    for pole in range(poles):
+    for load in loads[2:]:
+        load.wait()
+
+    for at in range(pieces):
         for step in range(1, row_count):
-            send_m(pole, step).wait_recv()
+            send_m(at, step).wait_recv()
+            if step == 1:
+                for index in ((), (1,), (), ())[at]:
+                    send_g(index).start()
 
             @pl.when(row == high)
             def _():
                 for across in range(1, row_count):
-                    send_x(pole, step, across).start()
+                    send_x(at, step, across).start()
 
     @pl.when(row != high)
     def _():
-        for pole in range(poles):
+        for at in range(pieces):
             for step in range(row_count):
-                send_x(pole, step, 1).wait_recv()
+                send_x(at, step, 1).wait_recv()
 
     def finish(index):
         cut = pl.ds(pl.multiple_of(index * chunk, chunk), chunk)
@@ -199,20 +236,30 @@
     def dot(left, right):
         return jnp.dot(left, right, preferred_element_type=jnp.float32)
 
+    def begin(index, carry):
+        cut = pl.ds(pl.multiple_of(index * chunk, chunk), chunk)
+        for sup in range(row_count):
+            for pole in range(poles):
+                m_own = jnp.concatenate(
+                    [panels[inner, sup, pole, 0, own_rows, :], panels[inner, sup, pole, 1, own_rows, :]], axis=1
+                )
+                for part in range(2):
+                    early[pole, sup, part, cut, :] = dot(inverse_ref[pole, part, cut, :], m_own)
+        return carry
+
+    lax.fori_loop(0, chunks, begin, 0)
+
     def work(index, carry):
         cut = pl.ds(pl.multiple_of(index * chunk, chunk), chunk)
         send_g(index).wait_recv()
         for sup in range(row_count):
             summed = None
             for pole in range(poles):
-                m_own = jnp.concatenate(
-                    [panels[inner, sup, pole, 0, own_rows, :], panels[inner, sup, pole, 1, own_rows, :]], axis=1
-                )
                 m_next = jnp.concatenate(
                     [panels[inner, sup, pole, 0, next_rows, :], panels[inner, sup, pole, 1, next_rows, :]], axis=1
                 )
-                by_re = dot(inverse_ref[pole, 0, cut, :], m_own) + dot(inverse_next[pole, 0, cut, :], m_next)
-                by_im = dot(inverse_ref[pole, 1, cut, :], m_own) + dot(inverse_next[pole, 1, cut, :], m_next)
+                by_re = early[pole, sup, 0, cut, :] + dot(inverse_next[pole, 0, cut, :], m_next)
+                by_im = early[pole, sup, 1, cut, :] + dot(inverse_next[pole, 1, cut, :], m_next)
                 solved_re = by_im[:, TILE:] - by_re[:, :TILE]
                 solved_im = -(by_re[:, TILE:] + by_im[:, :TILE])
                 w_re, w_im = weight_ref[pole, 0], weight_ref[pole, 1]
@@ -233,8 +280,11 @@
                 )
             total[sup, cut, :] = summed
             panel_send[index, sup] = summed.astype(jnp.bfloat16)
-        for step in range(1, row_count):
-            send_p(index, step).start()
+
+        @pl.when(index < chunks - 1)
+        def _():
+            for step in range(1, row_count):
+                send_p(index, step).start()
 
         @pl.when(index >= 1)
         def _():
@@ -245,18 +295,20 @@
     lax.fori_loop(0, chunks, work, 0)
 
     for sup in range(row_count):
-        quad_send[sup] = quad[sup, :, :TILE] + quad[sup, :, TILE:]
+        quad_send[sup] = (quad[sup, :, :TILE] + quad[sup, :, TILE:]).astype(jnp.bfloat16)
     for step in range(1, row_count):
         send_q(step).start()
+    for step in range(1, row_count):
+        send_p(chunks - 1, step).start()
     once = jnp.where(row == 0, 1.0, 0.0)
-    share = quad_send[high]
+    share = quad[high, :, :TILE] + quad[high, :, TILE:]
     for pole in range(poles):
         share = share + (once * weight_ref[pole, 0]) * diag_ref[pole, 0, 0]
         share = share - (once * weight_ref[pole, 1]) * diag_ref[pole, 1, 0]
     finish(chunks - 1)
     for step in range(1, row_count):
         send_q(step).wait_recv()
-        share = share + quad_recv[step - 1]
+        share = share + quad_recv[step - 1].astype(jnp.float32)
     shares[row, core] = share
     for which in range(len(others)):
         send_s(which).start()
@@ -270,16 +322,16 @@
         value = value + shares[at // 2, at % 2]
     diag_out[0] = value
 
-    for pole in range(poles):
+    for at in range(pieces):
         for step in range(1, row_count):
-            send_m(pole, step).wait_send()
+            send_m(at, step).wait_send()
 
     @pl.when(row == high)
     def _():
-        for pole in range(poles):
+        for at in range(pieces):
             for step in range(row_count):
                 for across in range(1, row_count):
-                    send_x(pole, step, across).wait_send()
+                    send_x(at, step, across).wait_send()
 
     for index in range(chunks):
         send_g(index).wait_send()
@@ -294,10 +346,10 @@
 
 def shards(row_count, inverse_block, lower_panel, tile_pattern, diag_inverse, pole_weight):
     poles, _, rows, half = inverse_block.shape
-    chunk = 128
+    chunk = 256
     chunks = rows // chunk
     vmem = pl.BlockSpec(memory_space=pltpu.VMEM)
-    smem = pl.BlockSpec(memory_space=pltpu.SMEM)
+    hbm = pl.BlockSpec(memory_space=pltpu.HBM)
     dma = pltpu.SemaphoreType.DMA
     bf16, f32 = jnp.bfloat16, jnp.float32
     steps = row_count - 1
@@ -308,9 +360,16 @@
             jax.ShapeDtypeStruct((rows, TILE), f32),
             jax.ShapeDtypeStruct((1, TILE, TILE), f32),
         ),
-        in_specs=[smem, smem, vmem, vmem, vmem],
+        in_specs=[hbm] * 5,
         out_specs=(vmem, vmem),
         scratch_shapes=[
+            pltpu.SMEM(tile_pattern.shape, jnp.int32),
+            pltpu.SMEM(pole_weight.shape, f32),
+            pltpu.VMEM(inverse_block.shape, bf16),
+            pltpu.VMEM(lower_panel.shape, bf16),
+            pltpu.VMEM(diag_inverse.shape, f32),
+            dma((5,)),
+            pltpu.VMEM((poles, row_count, 2, rows, 2 * TILE), f32),
             pltpu.VMEM((2, row_count, poles, 2, rows, TILE), bf16),
             pltpu.VMEM((poles, 2, rows, half), bf16),
             pltpu.VMEM((row_count, rows, TILE), f32),
@@ -319,13 +378,13 @@
             pltpu.VMEM((chunks, chunk, TILE), f32),
             pltpu.VMEM((chunks, chunk, TILE), f32),
             pltpu.VMEM((row_count, TILE, 2 * TILE), f32),
-            pltpu.VMEM((row_count, TILE, TILE), f32),
-            pltpu.VMEM((steps, TILE, TILE), f32),
+            pltpu.VMEM((row_count, TILE, TILE), bf16),
+            pltpu.VMEM((steps, TILE, TILE), bf16),
             pltpu.VMEM((row_count, 2, TILE, TILE), f32),
-            dma((steps, poles)),
-            dma((steps, poles)),
-            dma((steps, row_count, poles)),
-            dma((row_count, poles)),
+            dma((steps, 2 * poles)),
+            dma((steps, 2 * poles)),
+            dma((steps, row_count, 2 * poles)),
+            dma((row_count, 2 * poles)),
             dma((chunks,)),
             dma((chunks,)),
             dma((chunks, steps)),
@@ -338,7 +397,7 @@
             dma((2 * row_count - 1,)),
         ],
         compiler_params=pltpu.CompilerParams(
-            collective_id=0, has_side_effects=True, vmem_limit_bytes=40 * 1024 * 1024
+            collective_id=0, has_side_effects=True, vmem_limit_bytes=62 * 1024 * 1024
         ),
         cost_estimate=pl.CostEstimate(flops=flops, bytes_accessed=4 * 1024 * 1024, transcendentals=0),
     )(tile_pattern, pole_weight, inverse_block, lower_panel, diag_inverse)

time: 61 us -> 55.2 us (0.905)
  the two profiles are of different devices: /device:TPU:13 before, /device:TPU:0 now
where the time goes in v2:
time: 55.2 us; the launch traced here: 54.9 us
  Pallas kernels  52 us (94%)
  local copies, waits for them, and re-layouts  2.33 us (4%)
  between operations  0.65 us (1%)
    pallas_call x1, Pallas kernels, shards(): pl.pallas_call(functools.partial(kernel, row_count, chunk), out_shape=(ja...  52 us
    unnamed x4, local copies, waits for them, and re-layouts  2.33 us

profile of v2, /device:TPU:0, one launch (start us, length us, event | category | flops | bytes accessed | tf_op | source)
XLA Modules:
  0.0 54.9 jit_solution(10310286765980847835)
XLA Ops:
  0.6 52.0 %shard_map.68 = (f32[512,128]{1,0:T(8,128)}, f32[1,128,128]{2,1,0:T(8,128)}) custom-call(s32[4,8]{1,0:T(4,128)} %pattern_hbm.1, f32[2,2]{1,0:T(2,128)} %weight_hbm.1, bf16[2,2,512,256]{3,2,1,0:T(8,128)(2,1)} %inverse_hbm.1, bf16[2,2,512,128]{3,2,1,0:T(8,128)(2,1)} %lower_hbm.1, f32[2,2,1,128,128]{4,3,2,1,0:T(8,128)} %diag_hbm.1), custom_call_target="tpu_custom_call" | custom-call | flops 1342177280 | bytes 4194304 | tf_op jit(solution)/shard_map/pallas_call | solution.py:357
  52.6 0.0 copy-start
  52.6 1.7 %copy.9 = f32[512,128]{1,0:T(8,128)} copy(f32[512,128]{1,0:T(8,128)} %get-tuple-element.4) | data formatting | bytes 524288
  54.3 0.0 copy-done
  54.3 0.6 %copy.10 = f32[1,128,128]{2,1,0:T(8,128)} copy(f32[1,128,128]{2,1,0:T(8,128)S(1)} %copy-done) | data formatting | bytes 131072
Async XLA Ops:
  52.6 1.7 %copy-start = (f32[1,128,128]{2,1,0:T(8,128)S(1)}, f32[1,128,128]{2,1,0:T(8,128)}, u32[]{:S(2)}) copy-start(f32[1,128,128]{2,1,0:T(8,128)} %get-tuple-element.5) | copy-start | bytes 196612

commit v3 on v2

--- a/solution.py
+++ b/solution.py
@@ -286,10 +286,6 @@
             for step in range(1, row_count):
                 send_p(index, step).start()
 
-        @pl.when(index >= 1)
-        def _():
-            finish(index - 1)
-
         return carry
 
     lax.fori_loop(0, chunks, work, 0)
@@ -305,13 +301,14 @@
     for pole in range(poles):
         share = share + (once * weight_ref[pole, 0]) * diag_ref[pole, 0, 0]
         share = share - (once * weight_ref[pole, 1]) * diag_ref[pole, 1, 0]
-    finish(chunks - 1)
     for step in range(1, row_count):
         send_q(step).wait_recv()
         share = share + quad_recv[step - 1].astype(jnp.float32)
     shares[row, core] = share
-    for which in range(len(others)):
+    for which in reversed(range(len(others))):
         send_s(which).start()
+    for index in range(chunks):
+        finish(index)
     for index in range(chunks):
         send_c(index).wait_recv()
         panel_out[index * chunk : (index + 1) * chunk, :] = final[index] + final_recv[index]

time: 55.2 us -> 54.2 us (0.982)
  Pallas kernels: 52 us -> 51.1 us
    pallas_call x1, Pallas kernels: 52 us -> 51.1 us  [shards(): pl.pallas_call(functools.partial(kernel, row_count, chunk), out_shape=(ja...]
where the time goes in v3:
time: 54.2 us; the launch traced here: 54.1 us
  Pallas kernels  51.1 us (94%)
  local copies, waits for them, and re-layouts  2.33 us (4%)
  between operations  0.65 us (1%)
    pallas_call x1, Pallas kernels, shards(): pl.pallas_call(functools.partial(kernel, row_count, chunk), out_shape=(ja...  51.1 us
    unnamed x4, local copies, waits for them, and re-layouts  2.33 us

profile of v3, /device:TPU:0, one launch (start us, length us, event | category | flops | bytes accessed | tf_op | source)
XLA Modules:
  0.0 54.1 jit_solution(8239283608039901976)
XLA Ops:
  0.6 51.1 %shard_map.68 = (f32[512,128]{1,0:T(8,128)}, f32[1,128,128]{2,1,0:T(8,128)}) custom-call(s32[4,8]{1,0:T(4,128)} %pattern_hbm.1, f32[2,2]{1,0:T(2,128)} %weight_hbm.1, bf16[2,2,512,256]{3,2,1,0:T(8,128)(2,1)} %inverse_hbm.1, bf16[2,2,512,128]{3,2,1,0:T(8,128)(2,1)} %lower_hbm.1, f32[2,2,1,128,128]{4,3,2,1,0:T(8,128)} %diag_hbm.1), custom_call_target="tpu_custom_call" | custom-call | flops 1342177280 | bytes 4194304 | tf_op jit(solution)/shard_map/pallas_call | solution.py:354
  51.7 0.0 copy-start
  51.8 1.7 %copy.9 = f32[512,128]{1,0:T(8,128)} copy(f32[512,128]{1,0:T(8,128)} %get-tuple-element.4) | data formatting | bytes 524288
  53.5 0.0 copy-done
  53.5 0.6 %copy.10 = f32[1,128,128]{2,1,0:T(8,128)} copy(f32[1,128,128]{2,1,0:T(8,128)S(1)} %copy-done) | data formatting | bytes 131072
Async XLA Ops:
  51.7 1.7 %copy-start = (f32[1,128,128]{2,1,0:T(8,128)S(1)}, f32[1,128,128]{2,1,0:T(8,128)}, u32[]{:S(2)}) copy-start(f32[1,128,128]{2,1,0:T(8,128)} %get-tuple-element.5) | copy-start | bytes 196612

commit v4 on v3

--- a/solution.py
+++ b/solution.py
@@ -70,9 +70,9 @@
         return {"grow": lax.rem(row + step, row_count)}
 
     def piece(at):
-        return at // 2, pl.ds((at % 2) * (rows // 2), rows // 2)
-
-    pieces = 2 * poles
+        return at, pl.ds(0, rows)
+
+    pieces = poles
 
     def send_m(at, step):
         pole, part = piece(at)
@@ -207,7 +207,7 @@
         for step in range(1, row_count):
             send_m(at, step).wait_recv()
             if step == 1:
-                for index in ((), (1,), (), ())[at]:
+                for index in ((1,), (), (), ())[at]:
                     send_g(index).start()
 
             @pl.when(row == high)

time: 54.2 us -> 54.1 us (level)
  no operation moved by 1% of the time
where the time goes in v4:
time: 54.1 us; the launch traced here: 53.9 us
  Pallas kernels  51 us (94%)
  local copies, waits for them, and re-layouts  2.33 us (4%)
  between operations  0.65 us (1%)
    pallas_call x1, Pallas kernels, shards(): pl.pallas_call(functools.partial(kernel, row_count, chunk), out_shape=(ja...  51 us
    unnamed x4, local copies, waits for them, and re-layouts  2.33 us

profile of v4, /device:TPU:0, one launch (start us, length us, event | category | flops | bytes accessed | tf_op | source)
XLA Modules:
  0.0 53.9 jit_solution(5764932211770428738)
XLA Ops:
  0.6 51.0 %shard_map.68 = (f32[512,128]{1,0:T(8,128)}, f32[1,128,128]{2,1,0:T(8,128)}) custom-call(s32[4,8]{1,0:T(4,128)} %pattern_hbm.1, f32[2,2]{1,0:T(2,128)} %weight_hbm.1, bf16[2,2,512,256]{3,2,1,0:T(8,128)(2,1)} %inverse_hbm.1, bf16[2,2,512,128]{3,2,1,0:T(8,128)(2,1)} %lower_hbm.1, f32[2,2,1,128,128]{4,3,2,1,0:T(8,128)} %diag_hbm.1), custom_call_target="tpu_custom_call" | custom-call | flops 1342177280 | bytes 4194304 | tf_op jit(solution)/shard_map/pallas_call | solution.py:354
  51.6 0.0 copy-start
  51.6 1.7 %copy.9 = f32[512,128]{1,0:T(8,128)} copy(f32[512,128]{1,0:T(8,128)} %get-tuple-element.4) | data formatting | bytes 524288
  53.3 0.0 copy-done
  53.3 0.6 %copy.10 = f32[1,128,128]{2,1,0:T(8,128)} copy(f32[1,128,128]{2,1,0:T(8,128)S(1)} %copy-done) | data formatting | bytes 131072
Async XLA Ops:
  51.6 1.7 %copy-start = (f32[1,128,128]{2,1,0:T(8,128)S(1)}, f32[1,128,128]{2,1,0:T(8,128)}, u32[]{:S(2)}) copy-start(f32[1,128,128]{2,1,0:T(8,128)} %get-tuple-element.5) | copy-start | bytes 196612
